TPU v7x, 32 devices: a whole 2x2x4 slice. The times are simulated.
32 devices in a mesh: group: 2 (over y), ctx: 8 (over z, x), chan: 2 (over core).
Axes of the slice: x: 2, y: 2, z: 4, core: 2. Of those that a mesh axis runs over, the one named last changes fastest.
Arguments:
- values: bfloat16 [2048, 4096], P(('group', 'ctx'), 'chan'), parts along dimension 0, may hold values from -6 to 6
- pre_gate: bfloat16 [2048, 4096], P(('group', 'ctx'), 'chan'), parts along dimension 0, may hold values from -6 to 6
- post_gate: bfloat16 [2048, 4096], P(('group', 'ctx'), 'chan'), parts along dimension 0, may hold values from -6 to 6
- filter_spectrum: float32 [2, 16, 128, 4096], P(None, 'ctx', None, 'chan'), may hold values from -9 to 9
- skip_gain: float32 [4096], P('chan'), may hold values from 0.5 to 2
- out_weight: bfloat16 [4096, 4096], P('ctx', 'chan'), may hold values from -0.09375 to 0.09375
Outputs:
- projected: bfloat16 [2048, 4096], P(('group', 'ctx'), 'chan'), parts along dimension 0
There are 2 independent parts, one for each index of `group`. A program takes and returns all parts, laid end to end along the dimension named above; an argument that names none is the same for every part. Nothing has to cross between parts.
All inputs are finite; a program needn't handle non-finite values.
Results may differ from a plain program's by a relative error of at most 0.0049.
Values may be sent and summed in bfloat16 or wider, within the bound.
A program may use at most 128 MiB of HBM per device.

v0:
```python
import math

import jax
import jax.numpy as jnp
from jax import lax
from jax.sharding import PartitionSpec as P

HIGH = lax.Precision.HIGHEST


def trig_table(left_count, right_count, modulus):
    left_ids = jnp.arange(left_count, dtype=jnp.int32)[:, None]
    right_ids = jnp.arange(right_count, dtype=jnp.int32)[None, :]
    angles = (left_ids * right_ids % modulus).astype(jnp.float32) * (2.0 * math.pi / modulus)
    return (jnp.cos(angles), jnp.sin(angles))


def rotate(real_part, imag_part, cosine, sine):
    return (real_part * cosine - imag_part * sine, real_part * sine + imag_part * cosine)


def apply_matrix(matrix, operand):
    return jnp.einsum("kt,...tc->...kc", matrix, operand, precision=HIGH)


def local_transform(real_part, imag_part, direction_sign):
    length_now = real_part.shape[-2]
    cosine, sine = trig_table(length_now, length_now, length_now)
    new_real = apply_matrix(cosine, real_part) - direction_sign * apply_matrix(sine, imag_part)
    new_imag = apply_matrix(cosine, imag_part) + direction_sign * apply_matrix(sine, real_part)
    return (new_real, new_imag)


def twiddle(real_part, imag_part, row_ids, freq_ids, full_length, direction_sign):
    angles = (
        (row_ids * freq_ids % full_length).astype(jnp.float32)
        * (2.0 * math.pi / full_length)
        * direction_sign
    )
    return rotate(real_part, imag_part, jnp.cos(angles), jnp.sin(angles))


def contract_rows(activations, weight_piece):
    return lax.dot_general(
        activations, weight_piece, (((1,), (1,)), ((), ())), preferred_element_type=jnp.float32
    )


def local(values, pre_gate, post_gate, filter_spectrum, skip_gain, out_weight):
    seq_rows, chan_width = values.shape
    ctx_size = lax.axis_size("ctx")
    ctx_index = lax.axis_index("ctx")
    slice_rows = seq_rows // ctx_size
    full_length = 2 * seq_rows * ctx_size
    gated_input = values.astype(jnp.float32) * pre_gate.astype(jnp.float32)
    blocks = lax.all_to_all(
        gated_input.reshape(1, seq_rows, chan_width), "ctx", split_axis=1, concat_axis=0, tiled=True
    )
    flat_blocks = blocks.reshape(ctx_size, slice_rows * chan_width)
    block_cos, block_sin = trig_table(2 * ctx_size, ctx_size, 2 * ctx_size)
    real_part = jnp.dot(block_cos, flat_blocks, precision=HIGH).reshape(
        2 * ctx_size, slice_rows, chan_width
    )
    imag_part = -jnp.dot(block_sin, flat_blocks, precision=HIGH).reshape(
        2 * ctx_size, slice_rows, chan_width
    )
    row_ids = (ctx_index * slice_rows + jnp.arange(slice_rows, dtype=jnp.int32)).reshape(
        1, slice_rows, 1
    )
    freq_ids = jnp.arange(2 * ctx_size, dtype=jnp.int32).reshape(2 * ctx_size, 1, 1)
    real_part, imag_part = twiddle(real_part, imag_part, row_ids, freq_ids, full_length, -1.0)
    columns = lax.all_to_all(
        jnp.stack([real_part, imag_part]), "ctx", split_axis=1, concat_axis=2, tiled=True
    )
    real_part, imag_part = local_transform(columns[0], columns[1], -1.0)
    filter_real = filter_spectrum[0]
    filter_imag = filter_spectrum[1]
    product_real = real_part * filter_real - imag_part * filter_imag
    product_imag = real_part * filter_imag + imag_part * filter_real
    product_real, product_imag = local_transform(product_real, product_imag, 1.0)
    own_freq = (2 * ctx_index + jnp.arange(2, dtype=jnp.int32)).reshape(2, 1, 1)
    all_rows = jnp.arange(seq_rows, dtype=jnp.int32).reshape(1, seq_rows, 1)
    product_real, product_imag = twiddle(
        product_real, product_imag, all_rows, own_freq, full_length, 1.0
    )
    returned_spec = lax.all_to_all(
        jnp.stack([product_real, product_imag]), "ctx", split_axis=2, concat_axis=1, tiled=True
    )
    back_cos, back_sin = trig_table(ctx_size, 2 * ctx_size, 2 * ctx_size)
    spec_real = returned_spec[0].reshape(2 * ctx_size, slice_rows * chan_width)
    spec_imag = returned_spec[1].reshape(2 * ctx_size, slice_rows * chan_width)
    block_out = jnp.dot(back_cos, spec_real, precision=HIGH) - jnp.dot(
        back_sin, spec_imag, precision=HIGH
    )
    block_out = block_out.reshape(ctx_size, slice_rows, chan_width)
    returned = lax.all_to_all(block_out, "ctx", split_axis=0, concat_axis=1, tiled=True)
    convolved = returned.reshape(seq_rows, chan_width) / full_length
    mixer = (post_gate.astype(jnp.float32) * (convolved + skip_gain[None, :] * gated_input)).astype(
        jnp.bfloat16
    )
    partial_value = contract_rows(mixer, lax.all_gather(out_weight, "ctx", axis=0, tiled=True))
    projected = lax.psum_scatter(partial_value, "chan", scatter_dimension=1, tiled=True).astype(
        jnp.bfloat16
    )
    return projected


def solution(mesh):
    return jax.shard_map(
        local,
        mesh=mesh,
        in_specs=(
            P(("group", "ctx"), "chan"),
            P(("group", "ctx"), "chan"),
            P(("group", "ctx"), "chan"),
            P(None, "ctx", None, "chan"),
            P("chan"),
            P("ctx", "chan"),
        ),
        out_specs=P(("group", "ctx"), "chan"),
        check_vma=False,
    )
```

profile of v0, /device:TPU:0, one launch (start us, length us, event | category | flops | bytes accessed | tf_op | source)
XLA Modules:
  0.0 494.8 jit_solution(5310260831522021848)
XLA Ops:
  9.6 7.3 %all-to-all-start = ((f32[1,128,2048]{2,0,1:T(1,128)}), f32[1,128,2048]{2,0,1:T(1,128)S(1)}, u32[]{:S(2)}, u32[]{:S(2)}) async-start(f32[1,128,2048]{2,0,1:T(1,128)} %reshape.177), calls=%async_computation | async-start | bytes 2097152 | tf_op jit(solution)/shard_map/all_to_all | solution.py:56
  17.0 48.0 %all-to-all-done = f32[1,128,2048]{2,0,1:T(1,128)S(1)} async-done(((f32[1,128,2048]{2,0,1:T(1,128)}), f32[1,128,2048]{2,0,1:T(1,128)S(1)}, u32[]{:S(2)}, u32[]{:S(2)}) %all-to-all-start) | async-done | bytes 1048608 | tf_op jit(solution)/shard_map/all_to_all | solution.py:56
  65.0 2.5 reduce
  69.6 2.3 subtract_bitcast_fusion.1
  72.4 4.4 copy.35
  76.8 8.4 %all-to-all-start.1 = ((f32[2,16,16,2048]{3,2,0,1:T(8,128)}), f32[2,16,16,2048]{3,2,0,1:T(8,128)}, u32[]{:S(2)}, u32[]{:S(2)}) async-start(f32[2,16,16,2048]{3,2,0,1:T(8,128)} %copy.35), calls=%async_computation.1 | async-start | bytes 8388608 | tf_op jit(solution)/shard_map/all_to_all | solution.py:72
  85.2 4.7 fusion.122
  91.9 3.4 copy.55
  95.4 182.9 %all-to-all-done.1 = f32[2,16,16,2048]{3,2,0,1:T(8,128)} async-done(((f32[2,16,16,2048]{3,2,0,1:T(8,128)}), f32[2,16,16,2048]{3,2,0,1:T(8,128)}, u32[]{:S(2)}, u32[]{:S(2)}) %all-to-all-start.1) | async-done | bytes 4194336 | tf_op jit(solution)/shard_map/all_to_all | solution.py:72
  278.3 2.5 copy.36
  281.7 3.6 fusion.21
  285.3 3.7 fusion.19
  288.9 3.7 fusion.3
  292.6 3.9 fusion.4
  296.6 2.1 fusion.15
  300.8 2.1 convolution_add_fusion
  303.0 2.7 subtract_bitcast_fusion
  305.6 2.2 pad_maximum_fusion.1
  307.9 7.4 %copy.45 = f32[2,2,128,2048]{3,1,0,2:T(2,128)} copy(f32[2,2,128,2048]{2,3,1,0:T(8,128)} %pad_maximum_fusion.1) | data formatting | bytes 8388608 | tf_op jit(solution)/shard_map/stack | solution.py:87
  315.2 110.0 %all_to_all.48 = f32[2,2,128,2048]{3,1,0,2:T(2,128)S(1)} all-to-all(f32[2,2,128,2048]{3,1,0,2:T(2,128)} %copy.45), channel_id=1, replica_groups=mesh['group'=2,'ctx'=8,'chan'=2] {'ctx'}, dimensions={2} | all-to-all | bytes 8388608 | tf_op jit(solution)/shard_map/all_to_all | solution.py:86
  425.2 2.4 copy.46
  433.9 29.5 %all_to_all.49 = f32[8,16,2048]{2,1,0:T(8,128)S(1)} all-to-all(f32[8,16,2048]{2,1,0:T(8,128)S(1)} %copy.49), channel_id=1, replica_groups=mesh['group'=2,'ctx'=8,'chan'=2] {'ctx'}, dimensions={0} | all-to-all | bytes 2097152 | tf_op jit(solution)/shard_map/all_to_all | solution.py:96
  463.9 12.7 %fusion.128 = f32[128,4096]{1,0:T(8,128)} fusion(bf16[128,2048]{1,0:T(8,128)(2,1)S(1)} %fusion.7, bf16[4096,2048]{1,0:T(8,128)(2,1)} %all-gather.2.cloned.1.call-done), kind=kOutput, calls=%fused_computation.148 | convolution fusion | flops 2147483648 | bytes 19398656 | tf_op jit(solution)/shard_map/dot_general | solution.py:44
  476.6 8.8 %reduce-scatter.2.cloned.1.call-done = f32[128,2048]{1,0:T(8,128)} async-done(((f32[128,4096]{1,0:T(8,128)}), f32[128,2048]{1,0:T(8,128)}) %reduce-scatter.2.cloned.1.call-update) | async-done | bytes 1048592 | tf_op jit(solution)/shard_map/reduce_scatter | solution.py:102
  (40 shorter events, 19.6 us)
Async XLA Ops:
  6.5 1.0 copy-start.2
  6.5 1.2 copy-start.1
  6.5 457.3 %all-gather.2.cloned.1.call-start = ((), (), s32[]{:S(2)}) async-start(), calls=%async_computation.5 | async-start | bytes 18874368 | tf_op jit(solution)/shard_map/all_gather | solution.py:101
  9.6 55.4 %all-to-all-start = ((f32[1,128,2048]{2,0,1:T(1,128)}), f32[1,128,2048]{2,0,1:T(1,128)S(1)}, u32[]{:S(2)}, u32[]{:S(2)}) async-start(f32[1,128,2048]{2,0,1:T(1,128)} %reshape.177), calls=%async_computation | async-start | bytes 2097152 | tf_op jit(solution)/shard_map/all_to_all | solution.py:56
  76.8 201.5 %all-to-all-start.1 = ((f32[2,16,16,2048]{3,2,0,1:T(8,128)}), f32[2,16,16,2048]{3,2,0,1:T(8,128)}, u32[]{:S(2)}, u32[]{:S(2)}) async-start(f32[2,16,16,2048]{3,2,0,1:T(8,128)} %copy.35), calls=%async_computation.1 | async-start | bytes 8388608 | tf_op jit(solution)/shard_map/all_to_all | solution.py:72
  85.2 400.3 %reduce-scatter.2.cloned.1.call-start = ((), (), s32[]{:S(2)}) async-start(), calls=%async_computation.6 | async-start | bytes 3145728 | tf_op jit(solution)/shard_map/reduce_scatter | solution.py:102
  288.9 3.7 copy-start
  433.9 29.6 %copy-start.3 = (bf16[128,2048]{1,0:T(8,128)(2,1)S(1)}, bf16[128,2048]{1,0:T(8,128)(2,1)}, u32[]{:S(2)}) copy-start(bf16[128,2048]{1,0:T(8,128)(2,1)} %param.8) | copy-start | bytes 1572868
  433.9 29.6 %copy-start.4 = (f32[2048]{0:T(1024)S(1)}, f32[2048]{0:T(1024)}, u32[]{:S(2)}) copy-start(f32[2048]{0:T(1024)} %param.10) | copy-start | bytes 24580
Sparse Core Ops, SparseCore 0:
  9.5 383.5 all-gather.1
  476.8 8.6 reduce-scatter.1
where the time goes:
time: 504 us; the launch traced here: 495 us
  waiting for transfers between devices  241 us (48%)
  blocking collectives  139 us (28%)
  matrix products  43 us (9%)
  local copies, waits for them, and re-layouts  34 us (7%)
  starting transfers between devices  15.7 us (3%)
  between operations  14.1 us (3%)
  other arithmetic  8.06 us (2%)
    all_to_all x1, waiting for transfers between devices, local(): lax.all_to_all(jnp.stack([real_part, imag_part]), 'ctx', split_axis=1, co...  183 us
    all_to_all x1, blocking collectives, local(): lax.all_to_all(jnp.stack([product_real, product_imag]), 'ctx', split_axis...  110 us
    all_to_all x1, waiting for transfers between devices, local(): lax.all_to_all(gated_input.reshape(1, seq_rows, chan_width), 'ctx', split...  48 us
    all_to_all x1, blocking collectives, local(): lax.all_to_all(block_out, 'ctx', split_axis=0, concat_axis=1, tiled=True)  29.5 us
    dot_general x8, matrix products, apply_matrix(): return jnp.einsum('kt,...tc->...kc', matrix, operand, precision=HIGH)  23.9 us
    dot_general x1, matrix products, contract_rows(): lax.dot_general(activations, weight_piece, (((1,), (1,)), ((), ())), pref...  12.7 us
  transfers between devices with their start and end apart: 4, of which 3 were waited for; matrix products, arithmetic and copies ran while one was open for 14% of the time, Pallas kernels for 0%

commit v1 on v0

--- a/solution.py
+++ b/solution.py
@@ -2,6 +2,7 @@
 
 import jax
 import jax.numpy as jnp
+import numpy as np
 from jax import lax
 from jax.sharding import PartitionSpec as P
 
@@ -105,9 +106,83 @@
     return projected
 
 
+def dft_tables(residues, quotients, positions):
+    full_length = residues * quotients
+    kept = residues // 2 + 1
+    freq = (np.arange(kept)[:, None] + residues * np.arange(quotients)[None, :]).reshape(-1, 1)
+    steps = (freq * np.arange(positions)[None, :]) % full_length
+    angles = steps * (2.0 * math.pi / full_length)
+    table = np.concatenate([np.cos(angles), -np.sin(angles)], axis=0).astype(np.float32)
+    high = table.astype(jnp.bfloat16)
+    low = (table - high.astype(np.float32)).astype(jnp.bfloat16)
+    return np.concatenate([high, low], axis=1)
+
+
+def spread(values, pre_gate, post_gate, filter_spectrum, skip_gain, out_weight):
+    f32, bf16 = jnp.float32, jnp.bfloat16
+    rows, width = values.shape
+    groups = lax.axis_size("group")
+    ctx_size = lax.axis_size("ctx")
+    residues, quotients = 2 * ctx_size, filter_spectrum.shape[2]
+    length = rows * ctx_size
+    full_length = 2 * length
+    mine = width // (groups * ctx_size)
+    group_index = lax.axis_index("group")
+    ctx_index = lax.axis_index("ctx")
+    half = width // groups
+    part = lax.dynamic_slice_in_dim(filter_spectrum, group_index * half, half, axis=3)
+    part = (part * (1.0 / full_length)).astype(bf16)
+    part = part.reshape(2, 2, quotients, ctx_size, mine).transpose(3, 0, 1, 2, 4)
+    part = lax.all_to_all(part, "ctx", split_axis=0, concat_axis=0, tiled=True)
+    gated = (values.astype(f32) * pre_gate.astype(f32)).astype(bf16)
+    pair = jnp.stack([gated, post_gate]).reshape(2, rows, groups * ctx_size, mine).transpose(2, 0, 1, 3)
+    pair = lax.all_to_all(pair, ("group", "ctx"), split_axis=0, concat_axis=0, tiled=True)
+    pair = pair.reshape(groups, ctx_size, 2, rows, mine).transpose(2, 1, 3, 0, 4)
+    pair = pair.reshape(2, length, groups * mine)
+    gated, gate = pair[0], pair[1]
+    skip = lax.dynamic_slice_in_dim(
+        skip_gain, group_index * half + ctx_index * mine, mine, axis=0
+    )
+    spec = part.transpose(1, 0, 2, 3, 4).reshape(2, residues, quotients, mine)
+    middle = residues // 2
+    flip = jnp.asarray(np.eye(quotients, dtype=np.float32)[::-1], bf16)
+    mirrored = jnp.einsum(
+        "qp,xrpc->xrqc", flip, spec[:, :middle:-1], preferred_element_type=f32
+    )
+    sign = jnp.asarray([1.0, -1.0], f32).reshape(2, 1, 1, 1)
+    spec = spec[:, : middle + 1].astype(f32)
+    spec = spec + sign * jnp.pad(mirrored, ((0, 0), (1, 1), (0, 0), (0, 0)))
+    spec = spec.reshape(2, (middle + 1) * quotients, 1, mine)
+    table = jnp.asarray(dft_tables(residues, quotients, length))
+    trans = jnp.dot(table, jnp.concatenate([gated, gated], axis=0), preferred_element_type=f32)
+    trans = trans.reshape(2, (middle + 1) * quotients, groups, mine)
+    product = jnp.stack(
+        [trans[0] * spec[0] - trans[1] * spec[1], trans[0] * spec[1] + trans[1] * spec[0]]
+    ).astype(bf16)
+    product = product.reshape(2 * (middle + 1) * quotients, groups * mine)
+    both = lax.dot_general(table, product, (((0,), (0,)), ((), ())), preferred_element_type=f32)
+    convolved = both[:length] + both[length:]
+    skip = jnp.tile(skip, groups)
+    mixer = (gate.astype(f32) * (convolved + skip[None, :] * gated.astype(f32))).astype(bf16)
+    mixer = mixer.reshape(length, groups, mine).transpose(1, 0, 2)
+    mixer = lax.all_to_all(mixer, "group", split_axis=0, concat_axis=0, tiled=True)
+    mixer = lax.all_gather(mixer, "ctx", axis=0)
+    mixer = mixer.transpose(2, 1, 0, 3).reshape(length, width)
+    partial_value = contract_rows(mixer, out_weight)
+    summed = lax.psum_scatter(partial_value, "chan", scatter_dimension=1, tiled=True).astype(bf16)
+    chans = lax.axis_size("chan")
+    feats = summed.shape[1]
+    summed = summed.reshape(ctx_size, rows, feats)
+    summed = lax.all_to_all(summed, "ctx", split_axis=0, concat_axis=0, tiled=True)
+    summed = summed.reshape(chans, ctx_size // chans, rows, feats)
+    summed = lax.all_to_all(summed, "chan", split_axis=0, concat_axis=0, tiled=True)
+    return summed.transpose(2, 1, 0, 3).reshape(rows, ctx_size // chans * chans * feats)
+
+
 def solution(mesh):
+    small = mesh.shape["ctx"] <= 8
     return jax.shard_map(
-        local,
+        spread if small else local,
         mesh=mesh,
         in_specs=(
             P(("group", "ctx"), "chan"),

time: 504 us -> 259 us (0.51)
  the two profiles are of different devices: /device:TPU:0 before, /device:TPU:24 now
where the time goes in v1:
time: 259 us; the launch traced here: 254 us
  waiting for transfers between devices  116 us (45%)
  local copies, waits for them, and re-layouts  48.9 us (19%)
  blocking collectives  33.7 us (13%)
  matrix products  19 us (7%)
  between operations  13.6 us (5%)
  starting transfers between devices  13.5 us (5%)
  other arithmetic  9.55 us (4%)
    all_gather x1, waiting for transfers between devices, spread(): mixer = lax.all_gather(mixer, 'ctx', axis=0)  70.7 us
    all_to_all x1, waiting for transfers between devices, spread(): lax.all_to_all(pair, ('group', 'ctx'), split_axis=0, concat_axis=0, tiled...  21.5 us
    all_to_all x1, blocking collectives, spread(): lax.all_to_all(summed, 'ctx', split_axis=0, concat_axis=0, tiled=True)  18.1 us
    all_to_all x1, waiting for transfers between devices, spread(): part = lax.all_to_all(part, 'ctx', split_axis=0, concat_axis=0, tiled=True)  13.4 us
    all_to_all x1, blocking collectives, spread(): lax.all_to_all(mixer, 'group', split_axis=0, concat_axis=0, tiled=True)  11.5 us
    another operation x1, local copies, waits for them, and re-layouts, spread(): jnp.stack([trans[0] * spec[0] - trans[1] * spec[1], trans[0] * spec[1] +...  11.3 us
    reduce_scatter x1, waiting for transfers between devices, spread(): lax.psum_scatter(partial_value, 'chan', scatter_dimension=1, tiled=True)  10.1 us
    unnamed x14, local copies, waits for them, and re-layouts  9.12 us
  transfers between devices with their start and end apart: 4, of which 4 were waited for; matrix products, arithmetic and copies ran while one was open for 5% of the time, Pallas kernels for 0%

profile of v1, /device:TPU:24, one launch (start us, length us, event | category | flops | bytes accessed | tf_op | source)
XLA Modules:
  0.0 254.0 jit_solution(4278636132052713903)
XLA Ops:
  6.5 3.3 %constant_dynamic-slice_fusion = f32[2,2,128,1024]{3,2,1,0:T(8,128)} fusion(f32[2,2,128,2048]{3,2,1,0:T(8,128)} %param.12, s32[]{:T(128)S(6)} %select_n.6), kind=kLoop, calls=%fused_computation.21 | loop fusion | bytes 4194308 | tf_op jit(solution)/shard_map/dynamic_slice | solution.py:133
  9.9 2.9 %copy.106 = f32[2,2,128,1024]{2,3,1,0:T(8,128)} copy(f32[2,2,128,1024]{3,2,1,0:T(8,128)} %constant_dynamic-slice_fusion) | data formatting | bytes 4194304
  15.9 6.0 %all-to-all-start.1 = ((bf16[8,2,2,128,128]{4,3,2,1,0:T(8,128)(2,1)}), bf16[8,2,2,128,128]{4,3,2,1,0:T(8,128)(2,1)S(1)}, u32[]{:S(2)}, u32[]{:S(2)}) async-start(bf16[8,2,2,128,128]{4,3,2,1,0:T(8,128)(2,1)} %copy.93), calls=%async_computation.1 | async-start | bytes 2097152 | tf_op jit(solution)/shard_map/all_to_all | solution.py:136
  21.9 2.1 copy.85
  24.0 2.1 copy.86
  26.0 2.0 copy.87
  31.6 13.4 %all-to-all-done.1 = bf16[8,2,2,128,128]{4,3,2,1,0:T(8,128)(2,1)S(1)} async-done(((bf16[8,2,2,128,128]{4,3,2,1,0:T(8,128)(2,1)}), bf16[8,2,2,128,128]{4,3,2,1,0:T(8,128)(2,1)S(1)}, u32[]{:S(2)}, u32[]{:S(2)}) %all-to-all-start.1) | async-done | bytes 1048608 | tf_op jit(solution)/shard_map/all_to_all | solution.py:136
  45.0 7.2 %all-to-all-start = ((bf16[16,2,128,128]{2,3,1,0:T(8,128)(2,1)}), bf16[16,2,128,128]{2,3,1,0:T(8,128)(2,1)}, u32[]{:S(2)}, u32[]{:S(2)}) async-start(bf16[16,2,128,128]{2,3,1,0:T(8,128)(2,1)} %copy.88), calls=%async_computation | async-start | bytes 2097152 | tf_op jit(solution)/shard_map/all_to_all | solution.py:139
  54.8 21.5 %all-to-all-done = bf16[16,2,128,128]{2,3,1,0:T(8,128)(2,1)} async-done(((bf16[16,2,128,128]{2,3,1,0:T(8,128)(2,1)}), bf16[16,2,128,128]{2,3,1,0:T(8,128)(2,1)}, u32[]{:S(2)}, u32[]{:S(2)}) %all-to-all-start) | async-done | bytes 1048608 | tf_op jit(solution)/shard_map/all_to_all | solution.py:139
  80.6 2.6 %copy.90 = f32[1,8,128,2,128]{2,1,4,3,0:T(8,128)} copy(f32[1,8,128,2,128]{4,2,0,1,3:T(8,128)} %get-tuple-element.12) | data formatting | bytes 2097152 | tf_op jit(solution)/shard_map/convert_element_type | solution.py:166
  83.2 3.8 %fusion.5 = f32[256,2304]{1,0:T(8,128)S(1)} fusion(bf16[2304,1024]{1,0:T(8,128)(2,1)} %constant.34, bf16[32,8,8,128]{3,2,1,0:T(8,128)(2,1)S(1)} %bitcast.65), kind=kOutput, calls=%fused_computation.19 | convolution fusion | flops 1207959552 | bytes 7602176 | tf_op jit(solution)/shard_map/dot_general | solution.py:157
  86.9 3.8 %fusion = f32[2304,256]{0,1:T(8,128)S(1)} fusion(f32[256,2304]{1,0:T(8,128)S(1)} %fusion.5, bf16[2304,1024]{1,0:T(8,128)(2,1)} %constant.35, bf16[32,8,8,128]{3,2,1,0:T(8,128)(2,1)S(1)} %bitcast.66), kind=kOutput, calls=%fused_computation.1 | convolution fusion | flops 1208549376 | bytes 9961472 | tf_op jit(solution)/shard_map/dot_general | solution.py:157
  92.3 2.7 %copy.95 = f32[1,1152,2,128]{3,1,2,0:T(8,128)} copy(f32[1,1152,2,128]{1,3,2,0:T(8,128)} %bitcast.69) | data formatting | bytes 2359296 | tf_op jit(solution)/shard_map/squeeze | solution.py:160
  95.0 2.7 %copy.96 = f32[1,1152,2,128]{3,1,2,0:T(8,128)} copy(f32[1,1152,2,128]{1,3,2,0:T(8,128)} %bitcast.68) | data formatting | bytes 2359296 | tf_op jit(solution)/shard_map/squeeze | solution.py:160
  97.7 2.1 subtract_convert_fusion
  99.9 11.3 %copy.99 = bf16[2,1152,2,128]{3,2,1,0:T(2,128)(2,1)S(1)} copy(bf16[2,1152,2,128]{3,1,2,0:T(8,128)(2,1)S(1)} %pad_maximum_fusion) | data formatting | bytes 2359296 | tf_op jit(solution)/shard_map/stack | solution.py:159
  111.2 5.3 %fusion.1 = f32[2048,256]{0,1:T(8,128)S(1)} fusion(bf16[2304,2048]{1,0:T(8,128)(2,1)} %constant.30.clone, bf16[288,8,2,128]{3,2,1,0:T(2,128)(2,1)S(1)} %bitcast.87), kind=kOutput, calls=%fused_computation.9 | convolution fusion | flops 2415919104 | bytes 12713984 | tf_op jit(solution)/shard_map/dot_general | solution.py:163
  117.2 11.5 %all_to_all.25 = bf16[2,1024,128]{2,1,0:T(8,128)(2,1)} all-to-all(bf16[2,1024,128]{2,1,0:T(8,128)(2,1)S(1)} %bitcast.83), channel_id=1, replica_groups=mesh['group'=2,'ctx'=8,'chan'=2] {'group'}, dimensions={0} | all-to-all | bytes 1048576 | tf_op jit(solution)/shard_map/all_to_all | solution.py:168
  128.9 70.7 %all-gather.3.cloned.1.call-done = bf16[16,1024,128]{2,1,0:T(8,128)(2,1)} async-done(((bf16[2,1024,128]{2,1,0:T(8,128)(2,1)}), bf16[16,1024,128]{2,1,0:T(8,128)(2,1)}) %all-gather.3.cloned.1.call-update) | async-done | bytes 4194320 | tf_op jit(solution)/shard_map/all_gather | solution.py:169
  199.5 6.3 %copy.101 = bf16[1024,2,8,128]{0,3,2,1:T(8,128)(2,1)} copy(bf16[1024,2,8,128]{3,0,1,2:T(8,128)(2,1)} %bitcast.72) | data formatting | bytes 8388608 | tf_op jit(solution)/shard_map/transpose | solution.py:170
  205.8 5.9 %fusion.9 = f32[1024,512]{1,0:T(8,128)} fusion(bf16[1024,2048]{0,1:T(8,128)(2,1)} %bitcast.73, bf16[512,2048]{1,0:T(8,128)(2,1)S(1)} %copy-done), kind=kOutput, calls=%fused_computation.25 | convolution fusion | flops 2147483648 | bytes 8388608 | tf_op jit(solution)/shard_map/dot_general | solution.py:45
  211.7 10.1 %reduce-scatter.2.cloned.1.call-done = f32[1024,256]{1,0:T(8,128)} async-done(((f32[1024,512]{1,0:T(8,128)}), f32[1024,256]{1,0:T(8,128)}) %reduce-scatter.2.cloned.1.call-update) | async-done | bytes 1048592 | tf_op jit(solution)/shard_map/reduce_scatter | solution.py:172
  223.1 18.1 %all_to_all.26 = bf16[8,128,256]{2,1,0:T(8,128)(2,1)S(1)} all-to-all(bf16[8,128,256]{2,1,0:T(8,128)(2,1)S(1)} %bitcast.81), channel_id=1, replica_groups=mesh['group'=2,'ctx'=8,'chan'=2] {'ctx'}, dimensions={0} | all-to-all | bytes 1048576 | tf_op jit(solution)/shard_map/all_to_all | solution.py:176
  241.6 4.2 %all_to_all.27 = bf16[2,4,128,256]{3,1,2,0:T(4,128)(2,1)S(1)} all-to-all(bf16[2,4,128,256]{3,1,2,0:T(4,128)(2,1)S(1)} %copy.102), channel_id=1, replica_groups=mesh['group'=2,'ctx'=8,'chan'=2] {'chan'}, dimensions={0} | all-to-all | bytes 1048576 | tf_op jit(solution)/shard_map/all_to_all | solution.py:178
  (36 shorter events, 19.0 us)
Async XLA Ops:
  6.5 199.3 %copy-start = (bf16[512,2048]{1,0:T(8,128)(2,1)S(1)}, bf16[512,2048]{1,0:T(8,128)(2,1)}, u32[]{:S(2)}) copy-start(bf16[512,2048]{1,0:T(8,128)(2,1)} %param.14) | copy-start | bytes 6291460
  15.9 29.1 %all-to-all-start.1 = ((bf16[8,2,2,128,128]{4,3,2,1,0:T(8,128)(2,1)}), bf16[8,2,2,128,128]{4,3,2,1,0:T(8,128)(2,1)S(1)}, u32[]{:S(2)}, u32[]{:S(2)}) async-start(bf16[8,2,2,128,128]{4,3,2,1,0:T(8,128)(2,1)} %copy.93), calls=%async_computation.1 | async-start | bytes 2097152 | tf_op jit(solution)/shard_map/all_to_all | solution.py:136
  31.6 21.6 %copy-start.3 = (bf16[128,128,1,1]{1,0,3,2:T(8,128)(2,1)S(1)}, bf16[128,128,1,1]{1,0,3,2:T(8,128)(2,1)}, u32[]{:S(2)}) copy-start(bf16[128,128,1,1]{1,0,3,2:T(8,128)(2,1)} %constant.36) | copy-start | bytes 98308
  45.0 31.4 %all-to-all-start = ((bf16[16,2,128,128]{2,3,1,0:T(8,128)(2,1)}), bf16[16,2,128,128]{2,3,1,0:T(8,128)(2,1)}, u32[]{:S(2)}, u32[]{:S(2)}) async-start(bf16[16,2,128,128]{2,3,1,0:T(8,128)(2,1)} %copy.88), calls=%async_computation | async-start | bytes 2097152 | tf_op jit(solution)/shard_map/all_to_all | solution.py:139
  52.2 1.2 copy-start.4
  52.2 147.3 %all-gather.3.cloned.1.call-start = ((), (), s32[]{:S(2)}) async-start(), calls=%async_computation.7 | async-start | bytes 4718592 | tf_op jit(solution)/shard_map/all_gather | solution.py:169
  92.3 5.4 %copy-start.2 = (f32[1,9,128,128]{3,2,1,0:T(8,128)S(1)}, f32[1,9,128,128]{3,2,1,0:T(8,128)}, u32[]{:S(2)}) copy-start(f32[1,9,128,128]{3,2,1,0:T(8,128)} %get-tuple-element.9) | copy-start | bytes 1769476
  111.2 5.3 %copy-start.1 = (f32[1,8,128,2,128]{2,1,4,3,0:T(8,128)S(1)}, f32[1,8,128,2,128]{2,1,4,3,0:T(8,128)}, u32[]{:S(2)}) copy-start(f32[1,8,128,2,128]{2,1,4,3,0:T(8,128)} %copy.90) | copy-start | bytes 3145732
  128.7 93.1 %reduce-scatter.2.cloned.1.call-start = ((), (), s32[]{:S(2)}) async-start(), calls=%async_computation.6 | async-start | bytes 3145728 | tf_op jit(solution)/shard_map/reduce_scatter | solution.py:172
Sparse Core Ops, SparseCore 0:
  128.8 70.7 all-gather.2
  211.9 9.8 reduce-scatter.1

commit v2 on v1

--- a/solution.py
+++ b/solution.py
@@ -1,12 +1,16 @@
+import functools
 import math
 
 import jax
 import jax.numpy as jnp
 import numpy as np
 from jax import lax
+from jax.experimental import pallas as pl
+from jax.experimental.pallas import tpu as pltpu
 from jax.sharding import PartitionSpec as P
 
 HIGH = lax.Precision.HIGHEST
+MESH = pl.DeviceIdType.MESH
 
 
 def trig_table(left_count, right_count, modulus):
@@ -104,6 +108,216 @@
         jnp.bfloat16
     )
     return projected
+
+
+PARTS = 4
+
+
+def project_kernel(
+    mixer_ref, weight_ref, out_ref, held, total, share, near, sent, landed,
+    y_send, y_recv, z_send, z_recv, own_send, own_recv, pass_send, pass_recv,
+    core_send, core_recv, end_send, end_recv, *, lines
+):
+    ctx_size, groups, length, mine = held.shape
+    group = lax.axis_index("group")
+    ctx = lax.axis_index("ctx")
+    core = lax.axis_index("chan")
+    z, x = ctx // 2, ctx % 2
+    step = length // PARTS
+    rows = length // ctx_size
+    feats = weight_ref.shape[0]
+    per_core = ctx_size // 2
+
+    def device(ctx_id, core_id):
+        return (group, ctx_id, core_id)
+
+    across = (1 - group, ctx, core)
+    beside = device(z * 2 + 1 - x, core)
+    sibling = device(ctx, 1 - core)
+
+    barrier = pltpu.get_barrier_semaphore()
+    pl.semaphore_signal(barrier, inc=1, device_id=across, device_id_type=MESH)
+    pl.semaphore_signal(barrier, inc=1, device_id=sibling, device_id_type=MESH)
+    for offset in range(1, ctx_size):
+        for core_id in range(2):
+            pl.semaphore_signal(
+                barrier, inc=1, device_id=device(lax.rem(ctx + offset, ctx_size), core_id),
+                device_id_type=MESH,
+            )
+    pl.semaphore_wait(barrier, 2 * ctx_size)
+
+    def remote(src, dst, send, recv, target):
+        return pltpu.make_async_remote_copy(
+            src_ref=src, dst_ref=dst, send_sem=send, recv_sem=recv, device_id=target,
+            device_id_type=MESH,
+        )
+
+    def span(part):
+        return pl.ds(part * step, step)
+
+    def y_copy(part):
+        return remote(
+            mixer_ref.at[1 - group, span(part)], held.at[ctx, group, span(part)],
+            y_send.at[part], y_recv.at[part], across,
+        )
+
+    def z_copy(offset, part):
+        return remote(
+            held.at[ctx, :, span(part)], held.at[ctx, :, span(part)],
+            z_send.at[offset - 1, part], z_recv.at[offset - 1, part],
+            device(lax.rem(z + offset, lines) * 2 + x, core),
+        )
+
+    def own_copy(part):
+        return remote(
+            held.at[ctx, :, span(part)], held.at[ctx, :, span(part)],
+            own_send.at[part], own_recv.at[part], beside,
+        )
+
+    def pass_copy(offset, part):
+        source = lax.rem(z + lines - offset, lines) * 2 + x
+        return remote(
+            held.at[source, :, span(part)], held.at[source, :, span(part)],
+            pass_send.at[offset - 1, part], pass_recv.at[offset - 1, part], beside,
+        )
+
+    def core_copy(part):
+        return remote(
+            share.at[part], near.at[part], core_send.at[part], core_recv.at[part], sibling
+        )
+
+    slot = lax.rem(ctx, per_core)
+    owner = ctx // per_core
+
+    def end_copy(part):
+        return remote(
+            sent.at[part], landed.at[slot], end_send.at[part], end_recv.at[slot],
+            device(2 * part + core, owner),
+        )
+
+    for part in range(PARTS):
+        y_copy(part).start()
+    for part in range(PARTS):
+        held[ctx, group, part * step : (part + 1) * step, :] = mixer_ref[
+            group, part * step : (part + 1) * step, :
+        ]
+    for part in range(PARTS):
+        y_copy(part).wait_recv()
+        for offset in (2, 1, 3):
+            z_copy(offset, part).start()
+        own_copy(part).start()
+
+    def relay(part):
+        for offset in (1, 3, 2):
+            z_copy(offset, part).wait_recv()
+            pass_copy(offset, part).start()
+
+    def multiply(part):
+        own_copy(part).wait_recv()
+        for offset in (1, 3, 2):
+            pass_copy(offset, part).wait_recv()
+        for source in range(ctx_size):
+            block = jnp.concatenate(
+                [held[source, g, part * step : (part + 1) * step, :] for g in range(groups)], axis=1
+            )
+            columns = jnp.concatenate(
+                [
+                    weight_ref[:, (g * ctx_size + source) * mine : (g * ctx_size + source + 1) * mine]
+                    for g in range(groups)
+                ],
+                axis=1,
+            )
+            term = contract_rows(block, columns)
+            if source == 0:
+                total[part] = term
+            else:
+                total[part] += term
+        share[part] = total[part, pl.ds(pl.multiple_of((1 - core) * rows, rows), rows), :]
+        core_copy(part).start()
+
+    def finish(part):
+        core_copy(part).wait_recv()
+        mine_part = total[part, pl.ds(pl.multiple_of(core * rows, rows), rows), :]
+        sent[part] = (mine_part + near[part]).astype(sent.dtype)
+        here = jnp.logical_and(ctx == 2 * part + core, core == owner)
+
+        @pl.when(here)
+        def _():
+            landed[slot] = sent[part]
+
+        @pl.when(jnp.logical_not(here))
+        def _():
+            end_copy(part).start()
+
+    relay(0)
+    relay(1)
+    multiply(0)
+    relay(2)
+    multiply(1)
+    finish(0)
+    relay(3)
+    multiply(2)
+    finish(1)
+    multiply(3)
+    finish(2)
+    finish(3)
+
+    for source in range(per_core):
+        from_here = jnp.logical_and(core * per_core + source == ctx, core == lax.rem(ctx, 2))
+
+        @pl.when(jnp.logical_not(from_here))
+        def _():
+            remote(
+                sent.at[0], landed.at[source], end_send.at[0], end_recv.at[source],
+                device(0, 0),
+            ).wait_recv()
+
+        out_ref[:, source * feats : (source + 1) * feats] = landed[source]
+
+    for part in range(PARTS):
+        y_copy(part).wait_send()
+        own_copy(part).wait_send()
+        core_copy(part).wait_send()
+        for offset in range(1, lines):
+            z_copy(offset, part).wait_send()
+            pass_copy(offset, part).wait_send()
+        here = jnp.logical_and(ctx == 2 * part + core, core == owner)
+
+        @pl.when(jnp.logical_not(here))
+        def _():
+            end_copy(part).wait_send()
+
+
+def project(mixer, weight, ctx_size):
+    groups, length, mine = mixer.shape
+    feats = weight.shape[0]
+    rows = length // ctx_size
+    lines = ctx_size // 2
+    dma = pltpu.SemaphoreType.DMA
+    return pl.pallas_call(
+        functools.partial(project_kernel, lines=lines),
+        out_shape=jax.ShapeDtypeStruct((rows, feats * ctx_size // 2), jnp.bfloat16),
+        in_specs=[pl.BlockSpec(memory_space=pltpu.VMEM)] * 2,
+        out_specs=pl.BlockSpec(memory_space=pltpu.VMEM),
+        scratch_shapes=[
+            pltpu.VMEM((ctx_size, groups, length, mine), jnp.bfloat16),
+            pltpu.VMEM((PARTS, length // PARTS, feats), jnp.float32),
+            pltpu.VMEM((PARTS, rows, feats), jnp.float32),
+            pltpu.VMEM((PARTS, rows, feats), jnp.float32),
+            pltpu.VMEM((PARTS, rows, feats), jnp.bfloat16),
+            pltpu.VMEM((ctx_size // 2, rows, feats), jnp.bfloat16),
+            dma((PARTS,)), dma((PARTS,)),
+            dma((lines - 1, PARTS)), dma((lines - 1, PARTS)),
+            dma((PARTS,)), dma((PARTS,)),
+            dma((lines - 1, PARTS)), dma((lines - 1, PARTS)),
+            dma((PARTS,)), dma((PARTS,)),
+            dma((PARTS,)), dma((ctx_size // 2,)),
+        ],
+        compiler_params=pltpu.CompilerParams(
+            collective_id=0, has_side_effects=True, vmem_limit_bytes=40 * 1024 * 1024
+        ),
+        name="project",
+    )(mixer, weight)
 
 
 def dft_tables(residues, quotients, positions):
@@ -165,18 +379,7 @@
     skip = jnp.tile(skip, groups)
     mixer = (gate.astype(f32) * (convolved + skip[None, :] * gated.astype(f32))).astype(bf16)
     mixer = mixer.reshape(length, groups, mine).transpose(1, 0, 2)
-    mixer = lax.all_to_all(mixer, "group", split_axis=0, concat_axis=0, tiled=True)
-    mixer = lax.all_gather(mixer, "ctx", axis=0)
-    mixer = mixer.transpose(2, 1, 0, 3).reshape(length, width)
-    partial_value = contract_rows(mixer, out_weight)
-    summed = lax.psum_scatter(partial_value, "chan", scatter_dimension=1, tiled=True).astype(bf16)
-    chans = lax.axis_size("chan")
-    feats = summed.shape[1]
-    summed = summed.reshape(ctx_size, rows, feats)
-    summed = lax.all_to_all(summed, "ctx", split_axis=0, concat_axis=0, tiled=True)
-    summed = summed.reshape(chans, ctx_size // chans, rows, feats)
-    summed = lax.all_to_all(summed, "chan", split_axis=0, concat_axis=0, tiled=True)
-    return summed.transpose(2, 1, 0, 3).reshape(rows, ctx_size // chans * chans * feats)
+    return project(mixer, out_weight, ctx_size)
 
 
 def solution(mesh):

time: 259 us -> 181 us (0.70); the launches traced: 254 us -> 181 us
  Pallas kernels: 0 us -> 78.6 us
  waiting for transfers between devices: 116 us -> 42.1 us
  blocking collectives: 33.7 us -> 0 us
  local copies, waits for them, and re-layouts: 48.9 us -> 30.8 us
  between operations: 13.6 us -> 0.28 us
  matrix products: 19 us -> 11 us
  other arithmetic: 9.55 us -> 4.54 us
    pallas_call x0 -> x1, Pallas kernels: none -> 78.6 us  [project(): pl.pallas_call(functools.partial(project_kernel, lines=lines), out_shape=...]
    all_gather x1 -> x0, waiting for transfers between devices: 70.7 us -> none  [spread(): mixer = lax.all_gather(mixer, 'ctx', axis=0)]
    all_to_all x3 -> x0, blocking collectives: 33.7 us -> none  [the longest x1 18.1 us: spread(): lax.all_to_all(summed, 'ctx', split_axis=0, concat_axis=0, tiled=True)]
    reduce_scatter x1 -> x0, waiting for transfers between devices: 10.1 us -> none  [spread(): lax.psum_scatter(partial_value, 'chan', scatter_dimension=1, tiled=True)]
    all_to_all x1, waiting for transfers between devices: 13.4 us -> 20.4 us  [spread(): part = lax.all_to_all(part, 'ctx', split_axis=0, concat_axis=0, tiled=True)]
    transpose x1 -> x0, local copies, waits for them, and re-layouts: 6.26 us -> none  [spread(): mixer = mixer.transpose(2, 1, 0, 3).reshape(length, width)]
    dot_general x1 -> x0, matrix products: 5.9 us -> none  [contract_rows(): lax.dot_general(activations, weight_piece, (((1,), (1,)), ((), ())), pref...]
    unnamed x14 -> x29, local copies, waits for them, and re-layouts: 9.12 us -> 5.45 us
  transfers between devices with their start and end apart: 4 -> 2, of which waited for: 4 -> 2; matrix products, arithmetic and copies ran while one was open for 5% -> 2% of each run, Pallas kernels for 0% -> 0%
where the time goes in v2:
time: 181 us
  Pallas kernels  78.6 us (43%)
  waiting for transfers between devices  42.1 us (23%)
  local copies, waits for them, and re-layouts  30.8 us (17%)
  starting transfers between devices  13.4 us (7%)
  matrix products  11 us (6%)
  other arithmetic  4.54 us (3%)
    pallas_call x1, Pallas kernels, project(): pl.pallas_call(functools.partial(project_kernel, lines=lines), out_shape=...  78.6 us
    all_to_all x1, waiting for transfers between devices, spread(): lax.all_to_all(pair, ('group', 'ctx'), split_axis=0, concat_axis=0, tiled...  21.7 us
    all_to_all x1, waiting for transfers between devices, spread(): part = lax.all_to_all(part, 'ctx', split_axis=0, concat_axis=0, tiled=True)  20.4 us
    another operation x1, local copies, waits for them, and re-layouts, spread(): jnp.stack([trans[0] * spec[0] - trans[1] * spec[1], trans[0] * spec[1] +...  11.3 us
    all_to_all x1, starting transfers between devices, spread(): lax.all_to_all(pair, ('group', 'ctx'), split_axis=0, concat_axis=0, tiled...  7.25 us
    all_to_all x1, starting transfers between devices, spread(): part = lax.all_to_all(part, 'ctx', split_axis=0, concat_axis=0, tiled=True)  6.16 us
    unnamed x29, local copies, waits for them, and re-layouts  5.45 us
    dot_general x2, matrix products, spread(): jnp.dot(table, jnp.concatenate([gated, gated], axis=0), preferred_element...  5.38 us
  transfers between devices with their start and end apart: 2, of which 2 were waited for; matrix products, arithmetic and copies ran while one was open for 2% of the time, Pallas kernels for 0%

profile of v2, /device:TPU:24, one launch (start us, length us, event | category | flops | bytes accessed | tf_op | source)
XLA Modules:
  0.0 180.7 jit_solution(838197770513728989)
XLA Ops:
  0.0 1.7 constant_dynamic-slice_fusion
  1.7 1.8 %copy.90 = f32[2,2,128,1024]{2,3,1,0:T(8,128)} copy(f32[2,2,128,1024]{3,2,1,0:T(8,128)S(1)} %constant_dynamic-slice_fusion) | data formatting | bytes 4194304
  3.6 1.8 multiply_convert_fusion
  5.4 1.3 copy.81
  6.7 6.2 %all-to-all-start.1 = ((bf16[8,2,2,128,128]{4,3,2,1,0:T(8,128)(2,1)}), bf16[8,2,2,128,128]{4,3,2,1,0:T(8,128)(2,1)S(1)}, u32[]{:S(2)}, u32[]{:S(2)}) async-start(bf16[8,2,2,128,128]{4,3,2,1,0:T(8,128)(2,1)} %copy.81), calls=%async_computation.1 | async-start | bytes 2097152 | tf_op jit(solution)/shard_map/all_to_all | solution.py:350
  14.4 1.1 copy.76
  15.5 20.4 %all-to-all-done.1 = bf16[8,2,2,128,128]{4,3,2,1,0:T(8,128)(2,1)S(1)} async-done(((bf16[8,2,2,128,128]{4,3,2,1,0:T(8,128)(2,1)}), bf16[8,2,2,128,128]{4,3,2,1,0:T(8,128)(2,1)S(1)}, u32[]{:S(2)}, u32[]{:S(2)}) %all-to-all-start.1) | async-done | bytes 1048608 | tf_op jit(solution)/shard_map/all_to_all | solution.py:350
  35.9 7.2 %all-to-all-start = ((bf16[16,2,128,128]{2,3,1,0:T(8,128)(2,1)}), bf16[16,2,128,128]{2,3,1,0:T(8,128)(2,1)S(1)}, u32[]{:S(2)}, u32[]{:S(2)}) async-start(bf16[16,2,128,128]{2,3,1,0:T(8,128)(2,1)} %copy.76), calls=%async_computation | async-start | bytes 2097152 | tf_op jit(solution)/shard_map/all_to_all | solution.py:353
  43.4 0.5 copy-done.8
  44.5 1.1 fusion.7
  45.6 21.7 %all-to-all-done = bf16[16,2,128,128]{2,3,1,0:T(8,128)(2,1)S(1)} async-done(((bf16[16,2,128,128]{2,3,1,0:T(8,128)(2,1)}), bf16[16,2,128,128]{2,3,1,0:T(8,128)(2,1)S(1)}, u32[]{:S(2)}, u32[]{:S(2)}) %all-to-all-start) | async-done | bytes 1048608 | tf_op jit(solution)/shard_map/all_to_all | solution.py:353
  67.2 0.7 copy.77
  68.4 1.3 copy.78
  69.7 3.9 %fusion.5 = f32[256,2304]{1,0:T(8,128)S(1)} fusion(bf16[2304,1024]{1,0:T(8,128)(2,1)} %constant.34, bf16[32,8,8,128]{3,2,1,0:T(8,128)(2,1)S(1)} %bitcast.55), kind=kOutput, calls=%fused_computation.19 | convolution fusion | flops 1207959552 | bytes 7602176 | tf_op jit(solution)/shard_map/dot_general | solution.py:371
  73.6 1.5 fusion
  75.1 1.6 fusion.6
  76.7 1.6 copy.83
  78.4 2.8 %copy.84 = f32[1,1152,2,128]{3,1,2,0:T(8,128)} copy(f32[1,1152,2,128]{1,3,2,0:T(8,128)} %bitcast.60) | data formatting | bytes 2359296 | tf_op jit(solution)/shard_map/squeeze | solution.py:374
  81.1 1.7 subtract_convert_fusion
  83.0 11.3 %copy.87 = bf16[2,1152,2,128]{3,2,1,0:T(2,128)(2,1)S(1)} copy(bf16[2,1152,2,128]{3,1,2,0:T(8,128)(2,1)S(1)} %pad_maximum_fusion) | data formatting | bytes 2359296 | tf_op jit(solution)/shard_map/stack | solution.py:373
  94.3 5.3 %fusion.1 = f32[2048,256]{0,1:T(8,128)S(1)} fusion(bf16[2304,2048]{1,0:T(8,128)(2,1)} %constant.30.clone, bf16[288,8,2,128]{3,2,1,0:T(2,128)(2,1)S(1)} %bitcast.73), kind=kOutput, calls=%fused_computation.9 | convolution fusion | flops 2415919104 | bytes 12713984 | tf_op jit(solution)/shard_map/dot_general | solution.py:377
  100.3 1.0 copy-done.1
  101.3 78.6 %project.1 = bf16[128,2048]{1,0:T(8,128)(2,1)S(1)} custom-call(bf16[2,1024,128]{2,1,0:T(8,128)(2,1)S(1)} %bitcast.54, bf16[512,2048]{1,0:T(8,128)(2,1)S(1)} %copy-done.1), custom_call_target="tpu_custom_call" | custom-call | tf_op jit(solution)/shard_map/project/pallas_call | solution.py:297
  179.9 0.8 copy.103
  (38 shorter events, 3.4 us)
Async XLA Ops:
  0.0 43.2 %copy-start = (f32[2048]{0:T(1024)S(1)}, f32[2048]{0:T(1024)}, u32[]{:S(2)}) copy-start(f32[2048]{0:T(1024)} %param.13) | copy-start | bytes 24580
  6.7 6.2 %copy-start.5 = (bf16[128,2048]{1,0:T(8,128)(2,1)S(1)}, bf16[128,2048]{1,0:T(8,128)(2,1)}, u32[]{:S(2)}) copy-start(bf16[128,2048]{1,0:T(8,128)(2,1)} %param.9) | copy-start | bytes 1572868
  6.7 6.4 %copy-start.6 = (bf16[128,2048]{1,0:T(8,128)(2,1)S(1)}, bf16[128,2048]{1,0:T(8,128)(2,1)}, u32[]{:S(2)}) copy-start(bf16[128,2048]{1,0:T(8,128)(2,1)} %param.10) | copy-start | bytes 1572868
  6.7 29.2 %all-to-all-start.1 = ((bf16[8,2,2,128,128]{4,3,2,1,0:T(8,128)(2,1)}), bf16[8,2,2,128,128]{4,3,2,1,0:T(8,128)(2,1)S(1)}, u32[]{:S(2)}, u32[]{:S(2)}) async-start(bf16[8,2,2,128,128]{4,3,2,1,0:T(8,128)(2,1)} %copy.81), calls=%async_computation.1 | async-start | bytes 2097152 | tf_op jit(solution)/shard_map/all_to_all | solution.py:350
  12.9 1.0 copy-start.7
  35.9 31.3 %all-to-all-start = ((bf16[16,2,128,128]{2,3,1,0:T(8,128)(2,1)}), bf16[16,2,128,128]{2,3,1,0:T(8,128)(2,1)S(1)}, u32[]{:S(2)}, u32[]{:S(2)}) async-start(bf16[16,2,128,128]{2,3,1,0:T(8,128)(2,1)} %copy.76), calls=%async_computation | async-start | bytes 2097152 | tf_op jit(solution)/shard_map/all_to_all | solution.py:353
  43.2 0.8 copy-start.8
  43.4 0.8 copy-start.9
  68.3 5.3 %slice-start = ((s8[4718592]{0:T(1024)(128)(4,1)}), s8[524288]{0:T(1024)(128)(4,1)S(1)}, s32[]{:S(2)}) async-start(s8[4718592]{0:T(1024)(128)(4,1)} %bitcast.58), calls=%async_computation.2 | async-start | bytes 1048576
  69.7 3.9 %slice-start.1 = ((s8[4718592]{0:T(1024)(128)(4,1)}), s8[4194304]{0:T(1024)(128)(4,1)S(1)}, s32[]{:S(2)}) async-start(s8[4718592]{0:T(1024)(128)(4,1)} %bitcast.58), calls=%async_computation.3 | async-start | bytes 8388608
  78.3 2.8 %copy-start.3 = (f32[1,9,128,128]{3,2,1,0:T(8,128)S(1)}, f32[1,9,128,128]{3,2,1,0:T(8,128)}, u32[]{:S(2)}) copy-start(f32[1,9,128,128]{3,2,1,0:T(8,128)} %get-tuple-element.9) | copy-start | bytes 1769476
  78.3 2.8 %copy-start.4 = (f32[1,9,128,128]{3,2,1,0:T(8,128)S(1)}, f32[1,9,128,128]{3,2,1,0:T(8,128)}, u32[]{:S(2)}) copy-start(f32[1,9,128,128]{3,2,1,0:T(8,128)} %get-tuple-element.10) | copy-start | bytes 1769476
  94.3 5.3 %copy-start.2 = (f32[1,8,128,2,128]{2,1,4,3,0:T(8,128)S(1)}, f32[1,8,128,2,128]{2,1,4,3,0:T(8,128)}, u32[]{:S(2)}) copy-start(f32[1,8,128,2,128]{2,1,4,3,0:T(8,128)} %copy.78) | copy-start | bytes 3145732
  99.7 1.6 copy-start.1

commit v3 on v2

--- a/solution.py
+++ b/solution.py
@@ -332,6 +332,150 @@
     return np.concatenate([high, low], axis=1)
 
 
+def convolve_kernel(
+    values_ref, pre_ref, post_ref, skip_ref, flip_ref, filter_ref, table_ref, back_ref, out_ref,
+    spec_in, table, back, x_out, g_out, f_out, x_all, g_all, f_all, gated, trans, product,
+    load, x_send, x_recv, g_send, g_recv, f_send, f_recv
+):
+    f32, bf16 = jnp.float32, jnp.bfloat16
+    groups, length, mine = out_ref.shape
+    quotients = flip_ref.shape[0]
+    ctx_size = f_all.shape[0]
+    peers = groups * ctx_size
+    rows = length // ctx_size
+    middle = ctx_size
+    half = ctx_size * mine
+    group = lax.axis_index("group")
+    ctx = lax.axis_index("ctx")
+    core = lax.axis_index("chan")
+    me = group * ctx_size + ctx
+
+    filter_load = pltpu.make_async_copy(
+        filter_ref.at[:, :, :, pl.ds(pl.multiple_of(group * half, half), half)], spec_in, load.at[0]
+    )
+    filter_load.start()
+    table_load = pltpu.make_async_copy(table_ref, table, load.at[1])
+    table_load.start()
+    back_load = pltpu.make_async_copy(back_ref, back, load.at[2])
+    back_load.start()
+
+    def device(offset):
+        to = lax.rem(me + offset, peers)
+        return (to // ctx_size, lax.rem(to, ctx_size), core)
+
+    barrier = pltpu.get_barrier_semaphore()
+    for offset in range(1, peers):
+        pl.semaphore_signal(barrier, inc=1, device_id=device(offset), device_id_type=MESH)
+    for peer in range(peers):
+        cols = slice(peer * mine, (peer + 1) * mine)
+        x_out[peer] = (values_ref[:, cols].astype(f32) * pre_ref[:, cols].astype(f32)).astype(bf16)
+    pl.semaphore_wait(barrier, peers - 1)
+
+    def peer_copy(src, dst, send, recv, offset):
+        return pltpu.make_async_remote_copy(
+            src_ref=src.at[lax.rem(me + offset, peers)], dst_ref=dst.at[me],
+            send_sem=send.at[offset - 1], recv_sem=recv.at[offset - 1],
+            device_id=device(offset), device_id_type=MESH,
+        )
+
+    def peer_wait(src, dst, send, recv, offset):
+        pltpu.make_async_remote_copy(
+            src_ref=src.at[0], dst_ref=dst.at[lax.rem(me + peers - offset, peers)],
+            send_sem=send.at[offset - 1], recv_sem=recv.at[offset - 1],
+            device_id=device(offset), device_id_type=MESH,
+        ).wait_recv()
+
+    def filter_copy(offset):
+        to = lax.rem(ctx + offset, ctx_size)
+        return pltpu.make_async_remote_copy(
+            src_ref=f_out.at[to], dst_ref=f_all.at[ctx],
+            send_sem=f_send.at[offset - 1], recv_sem=f_recv.at[offset - 1],
+            device_id=(group, to, core), device_id_type=MESH,
+        )
+
+    def filter_wait(offset):
+        pltpu.make_async_remote_copy(
+            src_ref=f_out.at[0], dst_ref=f_all.at[lax.rem(ctx + ctx_size - offset, ctx_size)],
+            send_sem=f_send.at[offset - 1], recv_sem=f_recv.at[offset - 1],
+            device_id=(group, lax.rem(ctx + offset, ctx_size), core), device_id_type=MESH,
+        ).wait_recv()
+
+    for offset in range(1, peers):
+        peer_copy(x_out, x_all, x_send, x_recv, offset).start()
+    filter_load.wait()
+    scale = 1.0 / (2 * length)
+    for peer in range(ctx_size):
+        f_out[peer] = (spec_in[:, :, :, peer * mine : (peer + 1) * mine] * scale).astype(bf16)
+    for offset in range(1, ctx_size):
+        filter_copy(offset).start()
+    for peer in range(peers):
+        g_out[peer] = post_ref[:, peer * mine : (peer + 1) * mine]
+    for offset in range(1, peers):
+        peer_copy(g_out, g_all, g_send, g_recv, offset).start()
+    x_all[me] = x_out[me]
+    g_all[me] = g_out[me]
+    f_all[ctx] = f_out[ctx]
+
+    for offset in range(1, peers):
+        peer_wait(x_out, x_all, x_send, x_recv, offset)
+    for block in range(ctx_size):
+        gated[block * rows : (block + 1) * rows, :] = jnp.concatenate(
+            [x_all[g * ctx_size + block] for g in range(groups)], axis=1
+        )
+    table_load.wait()
+    kept = 2 * (middle + 1)
+
+    def forward(row, carry):
+        at = pl.ds(pl.multiple_of(row * quotients, quotients), quotients)
+        trans[at, :] = jnp.dot(
+            table[at, :length], gated[...], preferred_element_type=f32
+        ) + jnp.dot(table[at, length:], gated[...], preferred_element_type=f32)
+        return carry
+
+    lax.fori_loop(0, kept, forward, 0)
+
+    for offset in range(1, ctx_size):
+        filter_wait(offset)
+    for residue in range(middle + 1):
+        spec = [f_all[residue // 2, part, residue % 2].astype(f32) for part in range(2)]
+        if 0 < residue < middle:
+            other = 2 * ctx_size - residue
+            for part in range(2):
+                mirrored = jnp.dot(
+                    flip_ref[...], f_all[other // 2, part, other % 2], preferred_element_type=f32
+                )
+                spec[part] = spec[part] + (mirrored if part == 0 else -mirrored)
+        spec_re, spec_im = (jnp.concatenate([s] * groups, axis=1) for s in spec)
+        at_re = slice(residue * quotients, (residue + 1) * quotients)
+        at_im = slice((middle + 1 + residue) * quotients, (middle + 2 + residue) * quotients)
+        re, im = trans[at_re, :], trans[at_im, :]
+        product[at_re, :] = (re * spec_re - im * spec_im).astype(bf16)
+        product[at_im, :] = (re * spec_im + im * spec_re).astype(bf16)
+
+    back_load.wait()
+    for offset in range(1, peers):
+        peer_wait(g_out, g_all, g_send, g_recv, offset)
+    depth = kept * quotients
+
+    def backward(block, carry):
+        at = pl.ds(pl.multiple_of(block * rows, rows), rows)
+        convolved = jnp.dot(
+            back[at, :depth], product[...], preferred_element_type=f32
+        ) + jnp.dot(back[at, depth:], product[...], preferred_element_type=f32)
+        whole = convolved + skip_ref[...] * gated[at, :].astype(f32)
+        for g in range(groups):
+            gate = g_all[g * ctx_size + block].astype(f32)
+            out_ref[g, at, :] = (gate * whole[:, g * mine : (g + 1) * mine]).astype(bf16)
+        return carry
+
+    lax.fori_loop(0, ctx_size, backward, 0)
+    for offset in range(1, peers):
+        peer_copy(x_out, x_all, x_send, x_recv, offset).wait_send()
+        peer_copy(g_out, g_all, g_send, g_recv, offset).wait_send()
+    for offset in range(1, ctx_size):
+        filter_copy(offset).wait_send()
+
+
 def spread(values, pre_gate, post_gate, filter_spectrum, skip_gain, out_weight):
     f32, bf16 = jnp.float32, jnp.bfloat16
     rows, width = values.shape
@@ -339,46 +483,47 @@
     ctx_size = lax.axis_size("ctx")
     residues, quotients = 2 * ctx_size, filter_spectrum.shape[2]
     length = rows * ctx_size
-    full_length = 2 * length
-    mine = width // (groups * ctx_size)
+    peers = groups * ctx_size
+    mine = width // peers
     group_index = lax.axis_index("group")
     ctx_index = lax.axis_index("ctx")
-    half = width // groups
-    part = lax.dynamic_slice_in_dim(filter_spectrum, group_index * half, half, axis=3)
-    part = (part * (1.0 / full_length)).astype(bf16)
-    part = part.reshape(2, 2, quotients, ctx_size, mine).transpose(3, 0, 1, 2, 4)
-    part = lax.all_to_all(part, "ctx", split_axis=0, concat_axis=0, tiled=True)
-    gated = (values.astype(f32) * pre_gate.astype(f32)).astype(bf16)
-    pair = jnp.stack([gated, post_gate]).reshape(2, rows, groups * ctx_size, mine).transpose(2, 0, 1, 3)
-    pair = lax.all_to_all(pair, ("group", "ctx"), split_axis=0, concat_axis=0, tiled=True)
-    pair = pair.reshape(groups, ctx_size, 2, rows, mine).transpose(2, 1, 3, 0, 4)
-    pair = pair.reshape(2, length, groups * mine)
-    gated, gate = pair[0], pair[1]
     skip = lax.dynamic_slice_in_dim(
-        skip_gain, group_index * half + ctx_index * mine, mine, axis=0
-    )
-    spec = part.transpose(1, 0, 2, 3, 4).reshape(2, residues, quotients, mine)
-    middle = residues // 2
-    flip = jnp.asarray(np.eye(quotients, dtype=np.float32)[::-1], bf16)
-    mirrored = jnp.einsum(
-        "qp,xrpc->xrqc", flip, spec[:, :middle:-1], preferred_element_type=f32
-    )
-    sign = jnp.asarray([1.0, -1.0], f32).reshape(2, 1, 1, 1)
-    spec = spec[:, : middle + 1].astype(f32)
-    spec = spec + sign * jnp.pad(mirrored, ((0, 0), (1, 1), (0, 0), (0, 0)))
-    spec = spec.reshape(2, (middle + 1) * quotients, 1, mine)
-    table = jnp.asarray(dft_tables(residues, quotients, length))
-    trans = jnp.dot(table, jnp.concatenate([gated, gated], axis=0), preferred_element_type=f32)
-    trans = trans.reshape(2, (middle + 1) * quotients, groups, mine)
-    product = jnp.stack(
-        [trans[0] * spec[0] - trans[1] * spec[1], trans[0] * spec[1] + trans[1] * spec[0]]
-    ).astype(bf16)
-    product = product.reshape(2 * (middle + 1) * quotients, groups * mine)
-    both = lax.dot_general(table, product, (((0,), (0,)), ((), ())), preferred_element_type=f32)
-    convolved = both[:length] + both[length:]
-    skip = jnp.tile(skip, groups)
-    mixer = (gate.astype(f32) * (convolved + skip[None, :] * gated.astype(f32))).astype(bf16)
-    mixer = mixer.reshape(length, groups, mine).transpose(1, 0, 2)
+        skip_gain, (group_index * ctx_size + ctx_index) * mine, mine, axis=0
+    )
+    skip = jnp.tile(skip, groups).reshape(1, groups * mine)
+    flip = jnp.asarray(np.eye(quotients, dtype=np.float32)[::-1].astype(bf16))
+    table = dft_tables(residues, quotients, length)
+    back = np.concatenate([table[:, :length].T, table[:, length:].T], axis=1)
+    depth = table.shape[0]
+    vmem, dma = pltpu.VMEM, pltpu.SemaphoreType.DMA
+    here, there = pl.BlockSpec(memory_space=pltpu.VMEM), pl.BlockSpec(memory_space=pl.ANY)
+    mixer = pl.pallas_call(
+        convolve_kernel,
+        out_shape=jax.ShapeDtypeStruct((groups, length, mine), bf16),
+        in_specs=[here] * 5 + [there] * 3,
+        out_specs=here,
+        scratch_shapes=[
+            vmem((2, 2, quotients, width // groups), f32),
+            vmem(table.shape, bf16),
+            vmem(back.shape, bf16),
+            vmem((peers, rows, mine), bf16),
+            vmem((peers, rows, mine), bf16),
+            vmem((ctx_size, 2, 2, quotients, mine), bf16),
+            vmem((peers, rows, mine), bf16),
+            vmem((peers, rows, mine), bf16),
+            vmem((ctx_size, 2, 2, quotients, mine), bf16),
+            vmem((length, groups * mine), bf16),
+            vmem((depth, groups * mine), f32),
+            vmem((depth, groups * mine), bf16),
+            dma((3,)),
+            dma((peers - 1,)), dma((peers - 1,)), dma((peers - 1,)), dma((peers - 1,)),
+            dma((ctx_size - 1,)), dma((ctx_size - 1,)),
+        ],
+        compiler_params=pltpu.CompilerParams(
+            collective_id=1, has_side_effects=True, vmem_limit_bytes=48 * 1024 * 1024
+        ),
+        name="convolve",
+    )(values, pre_gate, post_gate, skip, flip, filter_spectrum, jnp.asarray(table), jnp.asarray(back))
     return project(mixer, out_weight, ctx_size)
 
 

time: 181 us -> 140 us (0.77)
  Pallas kernels: 78.6 us -> 134 us
  waiting for transfers between devices: 42.1 us -> 0 us
  local copies, waits for them, and re-layouts: 30.8 us -> 5.44 us
  starting transfers between devices: 13.4 us -> 0 us
  matrix products: 11 us -> 0 us
  other arithmetic: 4.54 us -> 0 us
    pallas_call x0 -> x1, Pallas kernels: none -> 54.8 us  [spread(): pl.pallas_call(convolve_kernel, out_shape=jax.ShapeDtypeStruct((groups, l...]
    all_to_all x2 -> x0, waiting for transfers between devices: 42.1 us -> none  [the longest x1 21.7 us: spread(): lax.all_to_all(pair, ('group', 'ctx'), split_axis=0, concat_axis=0, tiled...]
    all_to_all x2 -> x0, starting transfers between devices: 13.4 us -> none  [the longest x1 7.25 us: spread(): lax.all_to_all(pair, ('group', 'ctx'), split_axis=0, concat_axis=0, tiled...]
    another operation x1, local copies, waits for them, and re-layouts: 11.3 us -> 0.01 us  [spread(): skip = jnp.tile(skip, groups).reshape(1, groups * mine)]
    dot_general x4 -> x0, matrix products: 11 us -> none  [the longest x2 5.38 us: spread(): jnp.dot(table, jnp.concatenate([gated, gated], axis=0), preferred_element...]
    squeeze x2 -> x0, local copies, waits for them, and re-layouts: 4.4 us -> none  [the longest x1 2.78 us: spread(): trans[1] * spec[1]]
    slice x3 -> x0, local copies, waits for them, and re-layouts: 3.01 us -> none  [the longest x1 1.59 us: spread(): trans[0] * spec[0] - trans[1] * spec[1]]
    transpose x3 -> x0, local copies, waits for them, and re-layouts: 2.5 us -> none  [the longest x1 1.34 us: spread(): part.reshape(2, 2, quotients, ctx_size, mine).transpose(3, 0, 1, 2, 4)]
  transfers between devices with their start and end apart: 2 -> 0, of which waited for: 2 -> 0; matrix products, arithmetic and copies ran while one was open for 2% -> 0% of each run, Pallas kernels for 0% -> 0%
where the time goes in v3:
time: 140 us
  Pallas kernels  134 us (96%)
  local copies, waits for them, and re-layouts  5.44 us (4%)
    pallas_call x1, Pallas kernels, project(): pl.pallas_call(functools.partial(project_kernel, lines=lines), out_shape=...  79.7 us
    pallas_call x1, Pallas kernels, spread(): pl.pallas_call(convolve_kernel, out_shape=jax.ShapeDtypeStruct((groups, l...  54.8 us
    unnamed x11, local copies, waits for them, and re-layouts  4.68 us

profile of v3, /device:TPU:24, one launch (start us, length us, event | category | flops | bytes accessed | tf_op | source)
XLA Modules:
  0.0 140.0 jit_solution(5214601187780357178)
XLA Ops:
  0.0 0.8 dynamic_slice.3
  0.8 0.0 copy-start.1
  0.8 1.0 copy-done.1
  1.8 0.0 copy-start.2
  1.8 1.0 copy-done.2
  2.8 0.0 copy-start.3
  2.9 1.0 copy-done.3
  3.9 0.0 copy-start.4
  3.9 0.8 copy-done.4
  4.7 0.0 copy-start
  4.7 54.8 %convolve.1.mixer_ref = bf16[2,1024,128]{2,1,0:T(8,128)(2,1)S(1)} custom-call(bf16[128,2048]{1,0:T(8,128)(2,1)S(1)} %copy-done.1, bf16[128,2048]{1,0:T(8,128)(2,1)S(1)} %copy-done.2, bf16[128,2048]{1,0:T(8,128)(2,1)S(1)} %copy-done.3, f32[1,256]{1,0:T(1,128)S(1)} %bitcast.1, bf16[128,128]{1,0:T(8,128)(2,1)S(1)} %copy-done.4, f32[2,2,128,2048]{3,2,1,0:T(8,128)} %filter_ref.1, ...), custom_call_target="tpu_custom_call" | custom-call | tf_op jit(solution)/shard_map/convolve/pallas_call | solution.py:500
  59.5 0.0 copy-done
  59.5 79.7 %project.1 = bf16[128,2048]{1,0:T(8,128)(2,1)S(1)} custom-call(bf16[2,1024,128]{2,1,0:T(8,128)(2,1)S(1)} %convolve.1.mixer_ref, bf16[512,2048]{1,0:T(8,128)(2,1)S(1)} %copy-done), custom_call_target="tpu_custom_call" | custom-call | tf_op jit(solution)/shard_map/project/pallas_call | solution.py:297
  139.2 0.8 copy.11
  (1 shorter events, 0.0 us)
Async XLA Ops:
  0.8 1.0 copy-start.1
  1.8 1.0 copy-start.2
  2.8 1.0 copy-start.3
  3.9 0.8 copy-start.4
  4.7 54.8 %copy-start = (bf16[512,2048]{1,0:T(8,128)(2,1)S(1)}, bf16[512,2048]{1,0:T(8,128)(2,1)}, u32[]{:S(2)}) copy-start(bf16[512,2048]{1,0:T(8,128)(2,1)} %weight_ref.1) | copy-start | bytes 6291460

commit v4 on v3

--- a/solution.py
+++ b/solution.py
@@ -161,12 +161,24 @@
             y_send.at[part], y_recv.at[part], across,
         )
 
-    def z_copy(offset, part):
+    def line_index(way, hop):
+        return lax.rem(z + (lines - hop if way == 0 else hop), lines) * 2 + x
+
+    def comes(way, hop):
+        return z >= hop if way == 0 else z + hop < lines
+
+    def goes_on(way):
+        return z + 1 < lines if way == 0 else z > 0
+
+    def line_copy(way, hop, part, source):
         return remote(
-            held.at[ctx, :, span(part)], held.at[ctx, :, span(part)],
-            z_send.at[offset - 1, part], z_recv.at[offset - 1, part],
-            device(lax.rem(z + offset, lines) * 2 + x, core),
-        )
+            held.at[source, :, span(part)], held.at[source, :, span(part)],
+            z_send.at[way * (lines - 1) + hop - 1, part],
+            z_recv.at[way * (lines - 1) + hop - 1, part],
+            device(line_index(1 - way, 1), core),
+        )
+
+    ways = [(hop, way) for hop in range(1, lines) for way in range(2)]
 
     def own_copy(part):
         return remote(
@@ -174,11 +186,13 @@
             own_send.at[part], own_recv.at[part], beside,
         )
 
-    def pass_copy(offset, part):
-        source = lax.rem(z + lines - offset, lines) * 2 + x
+    def pass_copy(way, hop, part):
+        source = line_index(way, hop)
         return remote(
             held.at[source, :, span(part)], held.at[source, :, span(part)],
-            pass_send.at[offset - 1, part], pass_recv.at[offset - 1, part], beside,
+            pass_send.at[way * (lines - 1) + hop - 1, part],
+            pass_recv.at[way * (lines - 1) + hop - 1, part],
+            beside,
         )
 
     def core_copy(part):
@@ -203,19 +217,40 @@
         ]
     for part in range(PARTS):
         y_copy(part).wait_recv()
-        for offset in (2, 1, 3):
-            z_copy(offset, part).start()
+        for way in range(2):
+
+            @pl.when(goes_on(way))
+            def _():
+                line_copy(way, 1, part, ctx).start()
+
         own_copy(part).start()
 
-    def relay(part):
-        for offset in (1, 3, 2):
-            z_copy(offset, part).wait_recv()
-            pass_copy(offset, part).start()
+    def relay(turn):
+        for hop, way in ways:
+            part = turn - (hop - 1)
+            if not 0 <= part < PARTS:
+                continue
+
+            @pl.when(comes(way, hop))
+            def _():
+                source = line_index(way, hop)
+                line_copy(way, hop, part, source).wait_recv()
+                if hop + 1 < lines:
+
+                    @pl.when(goes_on(way))
+                    def _():
+                        line_copy(way, hop + 1, part, source).start()
+
+                pass_copy(way, hop, part).start()
 
     def multiply(part):
         own_copy(part).wait_recv()
-        for offset in (1, 3, 2):
-            pass_copy(offset, part).wait_recv()
+        for hop, way in ways:
+
+            @pl.when(comes(way, hop))
+            def _():
+                pass_copy(way, hop, part).wait_recv()
+
         for source in range(ctx_size):
             block = jnp.concatenate(
                 [held[source, g, part * step : (part + 1) * step, :] for g in range(groups)], axis=1
@@ -249,18 +284,19 @@
         def _():
             end_copy(part).start()
 
-    relay(0)
-    relay(1)
-    multiply(0)
-    relay(2)
-    multiply(1)
-    finish(0)
-    relay(3)
-    multiply(2)
-    finish(1)
-    multiply(3)
-    finish(2)
-    finish(3)
+    for turn in range(lines - 1):
+        relay(turn)
+    multiply_at = 0
+    for turn in range(lines - 1, PARTS + lines - 2):
+        relay(turn)
+        multiply(multiply_at)
+        if multiply_at:
+            finish(multiply_at - 1)
+        multiply_at += 1
+    for part in range(multiply_at, PARTS):
+        multiply(part)
+        finish(part - 1)
+    finish(PARTS - 1)
 
     for source in range(per_core):
         from_here = jnp.logical_and(core * per_core + source == ctx, core == lax.rem(ctx, 2))
@@ -278,9 +314,16 @@
         y_copy(part).wait_send()
         own_copy(part).wait_send()
         core_copy(part).wait_send()
-        for offset in range(1, lines):
-            z_copy(offset, part).wait_send()
-            pass_copy(offset, part).wait_send()
+        for hop, way in ways:
+
+            @pl.when(comes(way, hop))
+            def _():
+                pass_copy(way, hop, part).wait_send()
+
+            @pl.when(jnp.logical_and(comes(way, hop - 1), goes_on(way)))
+            def _():
+                line_copy(way, hop, part, line_index(way, hop - 1)).wait_send()
+
         here = jnp.logical_and(ctx == 2 * part + core, core == owner)
 
         @pl.when(jnp.logical_not(here))
@@ -307,9 +350,9 @@
             pltpu.VMEM((PARTS, rows, feats), jnp.bfloat16),
             pltpu.VMEM((ctx_size // 2, rows, feats), jnp.bfloat16),
             dma((PARTS,)), dma((PARTS,)),
-            dma((lines - 1, PARTS)), dma((lines - 1, PARTS)),
+            dma((2 * (lines - 1), PARTS)), dma((2 * (lines - 1), PARTS)),
             dma((PARTS,)), dma((PARTS,)),
-            dma((lines - 1, PARTS)), dma((lines - 1, PARTS)),
+            dma((2 * (lines - 1), PARTS)), dma((2 * (lines - 1), PARTS)),
             dma((PARTS,)), dma((PARTS,)),
             dma((PARTS,)), dma((ctx_size // 2,)),
         ],

time: 140 us -> 134 us (0.957)
  Pallas kernels: 134 us -> 128 us
    pallas_call x1, Pallas kernels: 79.7 us -> 73.7 us  [project(): pl.pallas_call(functools.partial(project_kernel, lines=lines), out_shape=...]
where the time goes in v4:
time: 134 us
  Pallas kernels  128 us (96%)
  local copies, waits for them, and re-layouts  5.44 us (4%)
    pallas_call x1, Pallas kernels, project(): pl.pallas_call(functools.partial(project_kernel, lines=lines), out_shape=...  73.7 us
    pallas_call x1, Pallas kernels, spread(): pl.pallas_call(convolve_kernel, out_shape=jax.ShapeDtypeStruct((groups, l...  54.8 us
    unnamed x11, local copies, waits for them, and re-layouts  4.68 us

profile of v4, /device:TPU:24, one launch (start us, length us, event | category | flops | bytes accessed | tf_op | source)
XLA Modules:
  0.0 133.9 jit_solution(14794354525181594903)
XLA Ops:
  0.0 0.8 dynamic_slice.3
  0.8 0.0 copy-start.1
  0.8 1.0 copy-done.1
  1.8 0.0 copy-start.2
  1.8 1.0 copy-done.2
  2.8 0.0 copy-start.3
  2.9 1.0 copy-done.3
  3.9 0.0 copy-start.4
  3.9 0.8 copy-done.4
  4.7 0.0 copy-start
  4.7 54.8 %convolve.1.mixer_ref = bf16[2,1024,128]{2,1,0:T(8,128)(2,1)S(1)} custom-call(bf16[128,2048]{1,0:T(8,128)(2,1)S(1)} %copy-done.1, bf16[128,2048]{1,0:T(8,128)(2,1)S(1)} %copy-done.2, bf16[128,2048]{1,0:T(8,128)(2,1)S(1)} %copy-done.3, f32[1,256]{1,0:T(1,128)S(1)} %bitcast.1, bf16[128,128]{1,0:T(8,128)(2,1)S(1)} %copy-done.4, f32[2,2,128,2048]{3,2,1,0:T(8,128)} %filter_ref.1, ...), custom_call_target="tpu_custom_call" | custom-call | tf_op jit(solution)/shard_map/convolve/pallas_call | solution.py:543
  59.5 0.0 copy-done
  59.5 73.7 %project.1 = bf16[128,2048]{1,0:T(8,128)(2,1)S(1)} custom-call(bf16[2,1024,128]{2,1,0:T(8,128)(2,1)S(1)} %convolve.1.mixer_ref, bf16[512,2048]{1,0:T(8,128)(2,1)S(1)} %copy-done), custom_call_target="tpu_custom_call" | custom-call | tf_op jit(solution)/shard_map/project/pallas_call | solution.py:340
  133.1 0.8 copy.11
  (1 shorter events, 0.0 us)
Async XLA Ops:
  0.8 1.0 copy-start.1
  1.8 1.0 copy-start.2
  2.8 1.0 copy-start.3
  3.9 0.8 copy-start.4
  4.7 54.8 %copy-start = (bf16[512,2048]{1,0:T(8,128)(2,1)S(1)}, bf16[512,2048]{1,0:T(8,128)(2,1)}, u32[]{:S(2)}) copy-start(bf16[512,2048]{1,0:T(8,128)(2,1)} %weight_ref.1) | copy-start | bytes 6291460
